TPU v7x, 32 devices: a whole 2x2x4 slice. The times are simulated.
32 devices in a mesh: file: 16 (over z, y, core), win: 2 (over x).
Axes of the slice: x: 2, y: 2, z: 4, core: 2. Of those that a mesh axis runs over, the one named last changes fastest.
Arguments:
- raw: bfloat16 [2, 128, 20480], P('win', None, 'file'), may hold values from -60 to 60
- fir_taps: float32 [64], replicated, may hold values from -0.75 to 0.75
- offsets: int32 [2, 16], P('win', 'file'), may hold values from 0 to 9
- vs_index: int32 [64], replicated, may hold values from 0 to 127, as said below
Outputs:
- correlation: float32 [64, 128, 2048], P('win', 'file')
Inputs may be any that keep to these rules, and one draw needn't show every extreme that they name: `vs_index`: virtual source s is one of the channels s * 2 to s * 2 + 1.
All inputs are finite; a program needn't handle non-finite values.
Results may differ from a plain program's by a relative error of at most 0.0063.
Values may be sent and summed in bfloat16 or wider, within the bound.
No kernel may reach another device: no remote copies, remote signals or barrier semaphores. Data moves between devices by JAX's collectives and lax.ppermute only.
A program may use at most 128 MiB of HBM per device.

v0:
```python
import math
import jax
import jax.numpy as jnp
from jax import lax
from jax.sharding import PartitionSpec as P

R = 10
TAPS = 64
TD = 128
SEG = 2048
BAND = 64
VS_DEV = 4
PRECISE = lax.Precision.HIGHEST
EPSILON = 1e-06


def phase_table(height, breadth, period_len):
    row_index = lax.broadcasted_iota(jnp.int32, (height, breadth), 0)
    col_index = lax.broadcasted_iota(jnp.int32, (height, breadth), 1)
    residue = row_index * col_index % period_len
    angles = residue.astype(jnp.float32) * (2.0 * math.pi / period_len)
    return (jnp.cos(angles), jnp.sin(angles))


def forward_spectrum(samples):
    length = samples.shape[-1]
    factor = min(128, length)
    inner = length // factor
    outer = 2 * length // factor
    half_factor = factor // 2
    leading = samples.shape[:-1]
    arranged = samples.astype(jnp.float32).reshape(leading + (inner, factor))
    cos_a, sin_a = phase_table(inner, outer, outer)
    first_re = jnp.einsum("...pa,pm->...ma", arranged, cos_a, precision=PRECISE)
    first_im = -jnp.einsum("...pa,pm->...ma", arranged, sin_a, precision=PRECISE)
    cos_t, sin_t = phase_table(outer, factor, 2 * length)
    twist_re = first_re * cos_t + first_im * sin_t
    twist_im = first_im * cos_t - first_re * sin_t
    cos_b, sin_b = phase_table(factor, half_factor, factor)
    out_re = jnp.einsum("...ma,an->...nm", twist_re, cos_b, precision=PRECISE) + jnp.einsum(
        "...ma,an->...nm", twist_im, sin_b, precision=PRECISE
    )
    out_im = jnp.einsum("...ma,an->...nm", twist_im, cos_b, precision=PRECISE) - jnp.einsum(
        "...ma,an->...nm", twist_re, sin_b, precision=PRECISE
    )
    return (out_re.reshape(leading + (length,)), out_im.reshape(leading + (length,)))


def inverse_lags(cross_re, cross_im):
    length = cross_re.shape[-1]
    factor = min(128, length)
    inner = length // factor
    outer = 2 * length // factor
    half_factor = factor // 2
    leading = cross_re.shape[:-1]
    quarter = jnp.arange(length, dtype=jnp.int32) % 4
    rotate_c = jnp.where(quarter == 0, 1.0, jnp.where(quarter == 2, -1.0, 0.0)).astype(jnp.float32)
    rotate_s = jnp.where(quarter == 1, 1.0, jnp.where(quarter == 3, -1.0, 0.0)).astype(jnp.float32)
    turned_re = (cross_re * rotate_c + cross_im * rotate_s).reshape(leading + (inner, factor))
    turned_im = (cross_im * rotate_c - cross_re * rotate_s).reshape(leading + (inner, factor))
    cos_a, sin_a = phase_table(inner, outer, outer)
    first_re = jnp.einsum("...pa,pm->...ma", turned_re, cos_a, precision=PRECISE) - jnp.einsum(
        "...pa,pm->...ma", turned_im, sin_a, precision=PRECISE
    )
    first_im = jnp.einsum("...pa,pm->...ma", turned_re, sin_a, precision=PRECISE) + jnp.einsum(
        "...pa,pm->...ma", turned_im, cos_a, precision=PRECISE
    )
    cos_t, sin_t = phase_table(outer, factor, 2 * length)
    twist_re = first_re * cos_t - first_im * sin_t
    twist_im = first_re * sin_t + first_im * cos_t
    cos_b, sin_b = phase_table(factor, half_factor, factor)
    lagged = jnp.einsum("...ma,an->...nm", twist_re, cos_b, precision=PRECISE) - jnp.einsum(
        "...ma,an->...nm", twist_im, sin_b, precision=PRECISE
    )
    return lagged.reshape(leading + (length,))


def whiten(spec_re, spec_im):
    length = spec_re.shape[-1]
    leading = spec_re.shape[:-1]
    magnitude = jnp.sqrt(spec_re * spec_re + spec_im * spec_im)
    amplitude = (
        jnp.mean(magnitude.reshape(leading + (length // BAND, BAND)), axis=-1, keepdims=True)
        + EPSILON
    )
    white_re = (spec_re.reshape(leading + (length // BAND, BAND)) / amplitude).reshape(
        leading + (length,)
    )
    white_im = (spec_im.reshape(leading + (length // BAND, BAND)) / amplitude).reshape(
        leading + (length,)
    )
    return (white_re.astype(jnp.bfloat16), white_im.astype(jnp.bfloat16))


def band_matrix(fir_taps, block_width):
    span = R * block_width + TAPS - R
    period_len = span + R
    flipped = fir_taps[::-1].astype(jnp.bfloat16)
    pattern = jnp.concatenate([flipped, jnp.zeros((period_len - TAPS,), jnp.bfloat16)])
    flat = jnp.tile(pattern, block_width)[: block_width * span]
    return flat.reshape(block_width, span).T


def decimate(extended, offset_now, band_taps):
    row_count = extended.shape[0]
    block_width = band_taps.shape[1]
    span = R * (TD - 1) + TAPS
    segment = lax.dynamic_slice_in_dim(extended, offset_now + 1, span, axis=1)
    block_count = TD // block_width
    stride_len = R * block_width
    leading_part = segment[:, : stride_len * block_count].reshape(
        row_count, block_count, stride_len
    )
    trailing = segment[:, stride_len:]
    trailing = jnp.pad(trailing, ((0, 0), (0, stride_len * block_count - trailing.shape[1])))
    trailing = trailing.reshape(row_count, block_count, stride_len)[:, :, : TAPS - R]
    blocks = jnp.concatenate([leading_part, trailing], axis=2)
    result = jnp.einsum("cbi,io->cbo", blocks, band_taps, preferred_element_type=jnp.float32)
    return result.reshape(row_count, TD)


def local(raw, fir_taps, offsets, vs_index):
    samples = raw[0]
    file_count = lax.axis_size("file")
    win_count = lax.axis_size("win")
    band_taps = band_matrix(fir_taps, math.gcd(TD, 128))
    regrouped = lax.all_to_all(samples, "file", split_axis=0, concat_axis=1, tiled=True)
    shifts = lax.all_gather(offsets, "file", axis=1, tiled=True)
    row_count = regrouped.shape[0]
    file_blocks = regrouped.reshape(row_count, file_count, regrouped.shape[1] // file_count)
    previous = jnp.concatenate(
        [
            jnp.zeros((row_count, 1, TAPS), file_blocks.dtype),
            file_blocks[:, :-1, file_blocks.shape[2] - TAPS :],
        ],
        axis=1,
    )
    extended = jnp.concatenate([previous, file_blocks], axis=2)
    pieces = jax.vmap(decimate, in_axes=(1, 0, None), out_axes=1)(extended, shifts[0], band_taps)
    owned = pieces.reshape(row_count, file_count * TD).astype(jnp.bfloat16)
    row_count = owned.shape[0]
    seg_count = owned.shape[1] // SEG
    own_re, own_im = forward_spectrum(owned.reshape(row_count, seg_count, SEG))
    white_re, white_im = whiten(own_re, own_im)
    file_pos = lax.axis_index("file")
    source_rows = (
        lax.dynamic_slice_in_dim(vs_index, file_pos * VS_DEV, VS_DEV) - file_pos * row_count
    )
    source_re, source_im = (
        lax.all_gather(jnp.take(white_re, source_rows, axis=0), "file", axis=0, tiled=True),
        lax.all_gather(jnp.take(white_im, source_rows, axis=0), "file", axis=0, tiled=True),
    )
    own_both = jnp.concatenate([white_re, white_im], axis=1)
    scale_out = 1.0 / math.sqrt(SEG * seg_count * win_count)
    paired = jnp.stack(
        [
            jnp.concatenate([source_re, source_im], axis=1),
            jnp.concatenate([-source_im, source_re], axis=1),
        ],
        axis=1,
    )
    joined = jnp.einsum("cqf,sdqf->scdf", own_both, paired, preferred_element_type=jnp.float32)
    stacked = lax.psum_scatter(
        joined.reshape(joined.shape[0], joined.shape[1], 2 * SEG),
        "win",
        scatter_dimension=0,
        tiled=True,
    )
    return inverse_lags(stacked[..., :SEG], stacked[..., SEG:]) * scale_out


def solution(mesh):
    return jax.shard_map(
        local,
        mesh=mesh,
        in_specs=(P("win", None, "file"), P(), P("win", "file"), P()),
        out_specs=P("win", "file", None),
        check_vma=False,
    )
```

profile of v0, /device:TPU:0, one launch (start us, length us, event | category | flops | bytes accessed | tf_op | source)
XLA Modules:
  0.0 293.7 jit_solution(40036436673634234)
XLA Ops:
  6.5 7.4 %all-to-all-start = ((bf16[16,8,1280]{2,1,0:T(8,128)(2,1)}), bf16[16,8,1280]{2,1,0:T(8,128)(2,1)S(1)}, u32[]{:S(2)}, u32[]{:S(2)}) async-start(bf16[16,8,1280]{2,1,0:T(8,128)(2,1)} %bitcast.144), calls=%async_computation | async-start | bytes 655360 | tf_op jit(solution)/shard_map/all_to_all | solution.py:127
  17.3 12.4 %all-reduce.4 = s32[16]{0:T(128)S(1)} all-reduce(s32[16]{0:T(128)S(1)} %bitcast_dynamic-update-slice_fusion), channel_id=1, replica_groups=mesh['file'=16,'win'=2] {'file'}, use_global_device_ids=true, to_apply=%add.4 | all-reduce | flops 16 | bytes 128
  31.9 29.9 %while.1 = (s32[]{:T(128)}, bf16[16,8,1344]{2,1,0:T(8,128)(2,1)S(1)}, s32[16,3]{0,1:T(4,128)S(1)}, bf16[16,8,1334]{2,1,0:T(8,128)(2,1)S(1)}, s32[]{:T(128)}) while((s32[]{:T(128)}, bf16[16,8,1344]{2,1,0:T(8,128)(2,1)S(1)}, s32[16,3]{0,1:T(4,128)S(1)}, bf16[16,8,1334]{2,1,0:T(8,128)(2,1)S(1)}, s32[]{:T(128)}) %tuple.29), condition=%wide.while_cond, body=%wide.while_body.sunk | while | flops 2 | bytes 45173 | solution.py:108
  32.5 1.3 dynamic-slice_dynamic-update-slice_fusion.2
  34.4 1.3 dynamic-slice_dynamic-update-slice_fusion.2
  41.9 1.3 dynamic-slice_dynamic-update-slice_fusion.2
  47.5 1.3 dynamic-slice_dynamic-update-slice_fusion.2
  53.1 1.3 dynamic-slice_dynamic-update-slice_fusion.2
  67.5 19.4 %all_gather.11 = bf16[64,1,2048]{2,1,0:T(2,128)(2,1)S(1)} all-gather(bf16[4,1,2048]{2,1,0:T(2,128)(2,1)S(1)} %copy.77), channel_id=1, replica_groups=mesh['file'=16,'win'=2] {'file'}, dimensions={0}, use_global_device_ids=true | all-gather | bytes 278528 | tf_op jit(solution)/shard_map/all_gather | solution.py:151
  87.1 19.7 %all_gather.10 = bf16[64,1,2048]{2,1,0:T(2,128)(2,1)S(1)} all-gather(bf16[4,1,2048]{2,1,0:T(2,128)(2,1)S(1)} %copy.75), channel_id=1, replica_groups=mesh['file'=16,'win'=2] {'file'}, dimensions={0}, use_global_device_ids=true | all-gather | bytes 278528 | tf_op jit(solution)/shard_map/all_gather | solution.py:150
  108.2 4.5 %copy.82 = bf16[64,2,2,2048]{0,2,1,3:T(2,128)(2,1)S(1)} copy(bf16[64,2,2,2048]{3,0,2,1:T(8,128)(2,1)} %pad_maximum_fusion) | data formatting | bytes 2097152 | tf_op jit(solution)/shard_map/stack | solution.py:155
  112.7 6.9 %convolution_bitcast_fusion = f32[64,8,2,2048]{0,1,2,3:T(8,128)} fusion(bf16[64,2,2,2048]{0,2,1,3:T(2,128)(2,1)S(1)} %copy.82, bf16[8,2,2048,1]{0,1,3,2:T(2,128)(2,1)S(1)} %copy.91), kind=kOutput, calls=%fused_computation.4 | convolution fusion | flops 8388608 | bytes 9502720 | tf_op jit(solution)/shard_map/cqf,sdqf->scdf/dot_general | solution.py:162
  119.6 17.3 %copy.84 = f32[64,8,2,2048]{3,2,1,0:T(2,128)} copy(f32[64,8,2,2048]{0,1,2,3:T(8,128)} %convolution_bitcast_fusion) | data formatting | bytes 16777216 | tf_op jit(solution)/shard_map/cqf,sdqf->scdf/transpose | solution.py:162
  136.8 11.8 %reshape.235 = f32[64,8,4096]{2,1,0:T(8,128)} reshape(f32[64,8,2,2048]{3,2,1,0:T(2,128)} %copy.84) | data formatting | bytes 16777216 | tf_op jit(solution)/shard_map/reshape | solution.py:164
  148.7 97.1 %reduce-scatter.2.cloned.1.call-done = f32[32,8,4096]{2,1,0:T(8,128)} async-done(((f32[64,8,4096]{2,1,0:T(8,128)}), f32[32,8,4096]{2,1,0:T(8,128)}) %reduce-scatter.2.cloned.1.call-update) | async-done | bytes 4194320 | tf_op jit(solution)/shard_map/reduce_scatter | solution.py:163
  245.8 2.8 subtract_bitcast_fusion
  248.6 3.5 %fusion.20 = f32[32,32,8,128]{3,0,2,1:T(8,128)S(1)} fusion(f32[32,8,16,128]{3,1,2,0:T(8,128)S(1)} %get-tuple-element.29), kind=kOutput, calls=%fused_computation.28 | convolution fusion | flops 201333760 | bytes 6291456 | tf_op jit(solution)/shard_map/...pa,pm->...ma/dot_general | solution.py:62
  252.1 3.7 %fusion.18 = f32[32,32,8,128]{3,0,2,1:T(8,128)S(1)} fusion(f32[32,8,16,128]{3,1,2,0:T(8,128)S(1)} %get-tuple-element.29), kind=kOutput, calls=%fused_computation.26 | convolution fusion | flops 201333760 | bytes 6291456 | tf_op jit(solution)/shard_map/...pa,pm->...ma/dot_general | solution.py:65
  255.8 3.6 %convolution_subtract_fusion = f32[32,32,8,128]{3,0,2,1:T(8,128)S(1)} fusion(f32[32,32,8,128]{3,0,2,1:T(8,128)S(1)} %fusion.20, f32[32,8,16,128]{3,1,2,0:T(8,128)S(1)} %get-tuple-element.28), kind=kOutput, calls=%fused_computation.17 | convolution fusion | flops 202382336 | bytes 10485760 | tf_op jit(solution)/shard_map/...pa,pm->...ma/dot_general | solution.py:62
  259.4 4.2 %convolution_add_fusion = f32[32,32,8,128]{3,0,2,1:T(8,128)S(1)} fusion(f32[32,32,8,128]{3,0,2,1:T(8,128)S(1)} %fusion.18, f32[32,8,16,128]{3,1,2,0:T(8,128)S(1)} %get-tuple-element.28), kind=kOutput, calls=%fused_computation.16 | convolution fusion | flops 202382336 | bytes 10485760 | tf_op jit(solution)/shard_map/...pa,pm->...ma/dot_general | solution.py:65
  263.6 3.5 %fusion = f32[64,32,8,32]{0,3,2,1:T(8,128)S(1)} fusion(f32[32,32,8,128]{3,0,2,1:T(8,128)S(1)} %convolution_add_fusion, f32[32,32,8,128]{3,0,2,1:T(8,128)S(1)} %convolution_subtract_fusion, f32[32,128]{1,0:T(8,128)S(1)} %get-tuple-element.38, f32[32,128]{1,0:T(8,128)S(1)} %get-tuple-element.39), kind=kOutput, calls=%fused_computation.5 | convolution fusion | flops 808566784 | bytes 10518528 | tf_op jit(solution)/shard_map/...ma,an->...nm/dot_general | solution.py:72
  267.1 5.3 %multiply_bitcast_fusion = f32[32,8,64,32]{2,3,1,0:T(8,128)} fusion(f32[64,32,8,32]{0,3,2,1:T(8,128)S(1)} %fusion, f32[32,32,8,128]{3,0,2,1:T(8,128)S(1)} %convolution_add_fusion, f32[32,32,8,128]{3,0,2,1:T(8,128)S(1)} %convolution_subtract_fusion, f32[32,128]{1,0:T(8,128)S(1)} %get-tuple-element.38, f32[32,128]{1,0:T(8,128)S(1)} %get-tuple-element.39), kind=kOutput, calls=%fused_computation.9 | convolution fusion | flops 809615360 | bytes 12615680 | tf_op jit(solution)/shard_map/...ma,an->...nm/dot_general | solution.py:72
  272.4 6.9 %copy.89 = f32[32,8,64,32]{3,2,1,0:T(8,128)} copy(f32[32,8,64,32]{2,3,1,0:T(8,128)} %multiply_bitcast_fusion) | data formatting | bytes 4194304 | tf_op jit(solution)/shard_map/mul | solution.py:169
  279.3 7.5 %mul.267 = f32[32,8,2048]{2,1,0:T(8,128)} reshape(f32[32,8,64,32]{3,2,1,0:T(8,128)} %copy.89) | data formatting | bytes 4194304 | tf_op jit(solution)/shard_map/mul | solution.py:169
  (98 shorter events, 35.5 us)
Async XLA Ops:
  6.5 25.1 %all-to-all-start = ((bf16[16,8,1280]{2,1,0:T(8,128)(2,1)}), bf16[16,8,1280]{2,1,0:T(8,128)(2,1)S(1)}, u32[]{:S(2)}, u32[]{:S(2)}) async-start(bf16[16,8,1280]{2,1,0:T(8,128)(2,1)} %bitcast.144), calls=%async_computation | async-start | bytes 655360 | tf_op jit(solution)/shard_map/all_to_all | solution.py:127
  13.9 231.8 %reduce-scatter.2.cloned.1.call-start = ((), (), s32[]{:S(2)}) async-start(), calls=%async_computation.2 | async-start | bytes 12582912 | tf_op jit(solution)/shard_map/reduce_scatter | solution.py:163
Sparse Core Ops, SparseCore 0:
  148.8 96.9 reduce-scatter.1
where the time goes:
time: 295 us; the launch traced here: 294 us
  waiting for transfers between devices  97.1 us (33%)
  local copies, waits for them, and re-layouts  84.7 us (29%)
  blocking collectives  51.5 us (17%)
  matrix products  33.2 us (11%)
  between operations  14.4 us (5%)
  starting transfers between devices  7.43 us (3%)
  other arithmetic  5.31 us (2%)
    reduce_scatter x1, waiting for transfers between devices, local(): lax.psum_scatter(joined.reshape(joined.shape[0], joined.shape[1], 2 * SEG...  97.1 us
    gather x48, local copies, waits for them, and re-layouts  29.9 us
    all_gather x1, blocking collectives, local(): lax.all_gather(jnp.take(white_re, source_rows, axis=0), 'file', axis=0, t...  19.7 us
    all_gather x1, blocking collectives, local(): lax.all_gather(jnp.take(white_im, source_rows, axis=0), 'file', axis=0, t...  19.4 us
    transpose x1, local copies, waits for them, and re-layouts, local(): jnp.einsum('cqf,sdqf->scdf', own_both, paired, preferred_element_type=jnp...  17.3 us
    mul x2, local copies, waits for them, and re-layouts, local(): return inverse_lags(stacked[..., :SEG], stacked[..., SEG:]) * scale_out  14.4 us
    unnamed x1, blocking collectives  12.4 us
    reshape x1, local copies, waits for them, and re-layouts, local(): joined.reshape(joined.shape[0], joined.shape[1], 2 * SEG)  11.8 us
  transfers between devices with their start and end apart: 2, of which 1 were waited for; matrix products, arithmetic and copies ran while one was open for 2% of the time, Pallas kernels for 0%

commit v1 on v0

--- a/solution.py
+++ b/solution.py
@@ -12,6 +12,18 @@
 VS_DEV = 4
 PRECISE = lax.Precision.HIGHEST
 EPSILON = 1e-06
+
+
+def doubled_up(x, axis, dim):
+    ways, here, step = (lax.axis_size(axis), lax.axis_index(axis), x.shape[dim])
+    line, have = (x, 1)
+    while have < ways:
+        line = jnp.concatenate(
+            [line, lax.ppermute(line, axis, [(d, (d - have) % ways) for d in range(ways)])],
+            axis=dim,
+        )
+        have = 2 * have
+    return jnp.roll(line, here * step, axis=dim)
 
 
 def phase_table(height, breadth, period_len):
@@ -147,7 +159,7 @@
         lax.dynamic_slice_in_dim(vs_index, file_pos * VS_DEV, VS_DEV) - file_pos * row_count
     )
     source_re, source_im = (
-        lax.all_gather(jnp.take(white_re, source_rows, axis=0), "file", axis=0, tiled=True),
+        doubled_up(jnp.take(white_re, source_rows, axis=0), "file", 0),
         lax.all_gather(jnp.take(white_im, source_rows, axis=0), "file", axis=0, tiled=True),
     )
     own_both = jnp.concatenate([white_re, white_im], axis=1)

time: 295 us -> 296 us (level)
  blocking collectives: 51.5 us -> 34.6 us
  waiting for transfers between devices: 97.1 us -> 111 us
  local copies, waits for them, and re-layouts: 84.7 us -> 87.8 us
    all_gather x1 -> x0, blocking collectives: 19.7 us -> none  [local(): lax.all_gather(jnp.take(white_re, source_rows, axis=0), 'file', axis=0, t...]
    ppermute x0 -> x4, waiting for transfers between devices: none -> 13.1 us  [doubled_up(): lax.ppermute(line, axis, [(d, (d - have) % ways) for d in range(ways)])]
    gather x48, local copies, waits for them, and re-layouts: 29.9 us -> 32.9 us
  transfers between devices with their start and end apart: 2 -> 6, of which waited for: 1 -> 4; matrix products, arithmetic and copies ran while one was open for 2% -> 2% of each run, Pallas kernels for 0% -> 0%
where the time goes in v1:
time: 296 us; the launch traced here: 295 us
  waiting for transfers between devices  111 us (38%)
  local copies, waits for them, and re-layouts  87.8 us (30%)
  blocking collectives  34.6 us (12%)
  matrix products  33.2 us (11%)
  between operations  14.4 us (5%)
  starting transfers between devices  8.48 us (3%)
  other arithmetic  5.4 us (2%)
    reduce_scatter x1, waiting for transfers between devices, local(): lax.psum_scatter(joined.reshape(joined.shape[0], joined.shape[1], 2 * SEG...  97.6 us
    gather x48, local copies, waits for them, and re-layouts  32.9 us
    all_gather x1, blocking collectives, local(): lax.all_gather(jnp.take(white_im, source_rows, axis=0), 'file', axis=0, t...  22.2 us
    transpose x1, local copies, waits for them, and re-layouts, local(): jnp.einsum('cqf,sdqf->scdf', own_both, paired, preferred_element_type=jnp...  17.3 us
    mul x2, local copies, waits for them, and re-layouts, local(): return inverse_lags(stacked[..., :SEG], stacked[..., SEG:]) * scale_out  14.4 us
    ppermute x4, waiting for transfers between devices, doubled_up(): lax.ppermute(line, axis, [(d, (d - have) % ways) for d in range(ways)])  13.1 us
    unnamed x1, blocking collectives  12.4 us
    reshape x1, local copies, waits for them, and re-layouts, local(): joined.reshape(joined.shape[0], joined.shape[1], 2 * SEG)  11.8 us
  transfers between devices with their start and end apart: 6, of which 4 were waited for; matrix products, arithmetic and copies ran while one was open for 2% of the time, Pallas kernels for 0%

profile of v1, /device:TPU:0, one launch (start us, length us, event | category | flops | bytes accessed | tf_op | source)
XLA Modules:
  0.0 294.7 jit_solution(6425315265659066422)
XLA Ops:
  6.5 7.4 %all-to-all-start = ((bf16[16,8,1280]{2,1,0:T(8,128)(2,1)}), bf16[16,8,1280]{2,1,0:T(8,128)(2,1)S(1)}, u32[]{:S(2)}, u32[]{:S(2)}) async-start(bf16[16,8,1280]{2,1,0:T(8,128)(2,1)} %bitcast.144), calls=%async_computation | async-start | bytes 655360 | tf_op jit(solution)/shard_map/all_to_all | solution.py:139
  17.3 12.4 %all-reduce.4 = s32[16]{0:T(128)S(1)} all-reduce(s32[16]{0:T(128)S(1)} %bitcast_dynamic-update-slice_fusion), channel_id=1, replica_groups=mesh['file'=16,'win'=2] {'file'}, use_global_device_ids=true, to_apply=%add.4 | all-reduce | flops 16 | bytes 128
  31.9 32.9 %while.1 = (s32[]{:T(128)}, bf16[16,8,1344]{2,1,0:T(8,128)(2,1)S(1)}, s32[16,3]{0,1:T(4,128)S(1)}, bf16[16,8,1334]{2,1,0:T(8,128)(2,1)S(1)}, s32[]{:T(128)}) while((s32[]{:T(128)}, bf16[16,8,1344]{2,1,0:T(8,128)(2,1)S(1)}, s32[16,3]{0,1:T(4,128)S(1)}, bf16[16,8,1334]{2,1,0:T(8,128)(2,1)S(1)}, s32[]{:T(128)}) %tuple.29), condition=%wide.while_cond, body=%wide.while_body.sunk | while | flops 2 | bytes 45173 | solution.py:120
  32.6 1.4 dynamic-slice_dynamic-update-slice_fusion.2
  34.7 1.4 dynamic-slice_dynamic-update-slice_fusion.2
  36.7 1.4 dynamic-slice_dynamic-update-slice_fusion.2
  38.8 1.4 dynamic-slice_dynamic-update-slice_fusion.2
  72.2 22.2 %all_gather.7 = bf16[64,1,2048]{2,1,0:T(2,128)(2,1)S(1)} all-gather(bf16[4,1,2048]{2,1,0:T(2,128)(2,1)S(1)} %copy.98), channel_id=1, replica_groups=mesh['file'=16,'win'=2] {'file'}, dimensions={0}, use_global_device_ids=true | all-gather | bytes 278528 | tf_op jit(solution)/shard_map/all_gather | solution.py:163
  94.7 4.2 %collective-permute-done.2 = bf16[16,1,2048]{2,0,1:T(8,128)(2,1)S(1)} collective-permute-done((bf16[16,1,2048]{2,0,1:T(8,128)(2,1)S(1)}, bf16[16,1,2048]{2,0,1:T(8,128)(2,1)S(1)}, u32[]{:S(2)}, u32[]{:S(2)}) %collective-permute-start.2) | collective-permute-done | bytes 65568 | tf_op jit(solution)/shard_map/ppermute | solution.py:22
  99.7 7.5 %collective-permute-done.3 = bf16[32,1,2048]{2,0,1:T(8,128)(2,1)S(1)} collective-permute-done((bf16[32,1,2048]{2,0,1:T(8,128)(2,1)S(1)}, bf16[32,1,2048]{2,0,1:T(8,128)(2,1)S(1)}, u32[]{:S(2)}, u32[]{:S(2)}) %collective-permute-start.3) | collective-permute-done | bytes 131104 | tf_op jit(solution)/shard_map/ppermute | solution.py:22
  108.6 4.5 %copy.101 = bf16[64,2,2,2048]{0,2,1,3:T(2,128)(2,1)S(1)} copy(bf16[64,2,2,2048]{3,0,2,1:T(8,128)(2,1)} %pad_maximum_fusion) | data formatting | bytes 2097152 | tf_op jit(solution)/shard_map/stack | solution.py:167
  113.2 6.9 %convolution_bitcast_fusion = f32[64,8,2,2048]{0,1,2,3:T(8,128)} fusion(bf16[64,2,2,2048]{0,2,1,3:T(2,128)(2,1)S(1)} %copy.101, bf16[8,2,2048,1]{0,1,3,2:T(2,128)(2,1)S(1)} %copy.110), kind=kOutput, calls=%fused_computation.4 | convolution fusion | flops 8388608 | bytes 9502720 | tf_op jit(solution)/shard_map/cqf,sdqf->scdf/dot_general | solution.py:174
  120.0 17.3 %copy.103 = f32[64,8,2,2048]{3,2,1,0:T(2,128)} copy(f32[64,8,2,2048]{0,1,2,3:T(8,128)} %convolution_bitcast_fusion) | data formatting | bytes 16777216 | tf_op jit(solution)/shard_map/cqf,sdqf->scdf/transpose | solution.py:174
  137.3 11.8 %reshape.235 = f32[64,8,4096]{2,1,0:T(8,128)} reshape(f32[64,8,2,2048]{3,2,1,0:T(2,128)} %copy.103) | data formatting | bytes 16777216 | tf_op jit(solution)/shard_map/reshape | solution.py:176
  149.2 97.6 %reduce-scatter.2.cloned.1.call-done = f32[32,8,4096]{2,1,0:T(8,128)} async-done(((f32[64,8,4096]{2,1,0:T(8,128)}), f32[32,8,4096]{2,1,0:T(8,128)}) %reduce-scatter.2.cloned.1.call-update) | async-done | bytes 4194320 | tf_op jit(solution)/shard_map/reduce_scatter | solution.py:175
  246.8 2.8 subtract_bitcast_fusion
  249.6 3.5 %fusion.20 = f32[32,32,8,128]{3,0,2,1:T(8,128)S(1)} fusion(f32[32,8,16,128]{3,1,2,0:T(8,128)S(1)} %get-tuple-element.29), kind=kOutput, calls=%fused_computation.28 | convolution fusion | flops 201333760 | bytes 6291456 | tf_op jit(solution)/shard_map/...pa,pm->...ma/dot_general | solution.py:74
  253.1 3.7 %fusion.18 = f32[32,32,8,128]{3,0,2,1:T(8,128)S(1)} fusion(f32[32,8,16,128]{3,1,2,0:T(8,128)S(1)} %get-tuple-element.29), kind=kOutput, calls=%fused_computation.26 | convolution fusion | flops 201333760 | bytes 6291456 | tf_op jit(solution)/shard_map/...pa,pm->...ma/dot_general | solution.py:77
  256.8 3.6 %convolution_subtract_fusion = f32[32,32,8,128]{3,0,2,1:T(8,128)S(1)} fusion(f32[32,32,8,128]{3,0,2,1:T(8,128)S(1)} %fusion.20, f32[32,8,16,128]{3,1,2,0:T(8,128)S(1)} %get-tuple-element.28), kind=kOutput, calls=%fused_computation.17 | convolution fusion | flops 202382336 | bytes 10485760 | tf_op jit(solution)/shard_map/...pa,pm->...ma/dot_general | solution.py:74
  260.4 4.2 %convolution_add_fusion = f32[32,32,8,128]{3,0,2,1:T(8,128)S(1)} fusion(f32[32,32,8,128]{3,0,2,1:T(8,128)S(1)} %fusion.18, f32[32,8,16,128]{3,1,2,0:T(8,128)S(1)} %get-tuple-element.28), kind=kOutput, calls=%fused_computation.16 | convolution fusion | flops 202382336 | bytes 10485760 | tf_op jit(solution)/shard_map/...pa,pm->...ma/dot_general | solution.py:77
  264.6 3.5 %fusion = f32[64,32,8,32]{0,3,2,1:T(8,128)S(1)} fusion(f32[32,32,8,128]{3,0,2,1:T(8,128)S(1)} %convolution_add_fusion, f32[32,32,8,128]{3,0,2,1:T(8,128)S(1)} %convolution_subtract_fusion, f32[32,128]{1,0:T(8,128)S(1)} %get-tuple-element.38, f32[32,128]{1,0:T(8,128)S(1)} %get-tuple-element.39), kind=kOutput, calls=%fused_computation.5 | convolution fusion | flops 808566784 | bytes 10518528 | tf_op jit(solution)/shard_map/...ma,an->...nm/dot_general | solution.py:84
  268.1 5.3 %multiply_bitcast_fusion = f32[32,8,64,32]{2,3,1,0:T(8,128)} fusion(f32[64,32,8,32]{0,3,2,1:T(8,128)S(1)} %fusion, f32[32,32,8,128]{3,0,2,1:T(8,128)S(1)} %convolution_add_fusion, f32[32,32,8,128]{3,0,2,1:T(8,128)S(1)} %convolution_subtract_fusion, f32[32,128]{1,0:T(8,128)S(1)} %get-tuple-element.38, f32[32,128]{1,0:T(8,128)S(1)} %get-tuple-element.39), kind=kOutput, calls=%fused_computation.9 | convolution fusion | flops 809615360 | bytes 12615680 | tf_op jit(solution)/shard_map/...ma,an->...nm/dot_general | solution.py:84
  273.4 6.9 %copy.108 = f32[32,8,64,32]{3,2,1,0:T(8,128)} copy(f32[32,8,64,32]{2,3,1,0:T(8,128)} %multiply_bitcast_fusion) | data formatting | bytes 4194304 | tf_op jit(solution)/shard_map/mul | solution.py:181
  280.4 7.5 %mul.268 = f32[32,8,2048]{2,1,0:T(8,128)} reshape(f32[32,8,64,32]{3,2,1,0:T(8,128)} %copy.108) | data formatting | bytes 4194304 | tf_op jit(solution)/shard_map/mul | solution.py:181
  (108 shorter events, 41.8 us)
Async XLA Ops:
  6.5 25.1 %all-to-all-start = ((bf16[16,8,1280]{2,1,0:T(8,128)(2,1)}), bf16[16,8,1280]{2,1,0:T(8,128)(2,1)S(1)}, u32[]{:S(2)}, u32[]{:S(2)}) async-start(bf16[16,8,1280]{2,1,0:T(8,128)(2,1)} %bitcast.144), calls=%async_computation | async-start | bytes 655360 | tf_op jit(solution)/shard_map/all_to_all | solution.py:139
  13.9 232.8 %reduce-scatter.2.cloned.1.call-start = ((), (), s32[]{:S(2)}) async-start(), calls=%async_computation.2 | async-start | bytes 12582912 | tf_op jit(solution)/shard_map/reduce_scatter | solution.py:175
  69.8 1.5 collective-permute-start
  71.3 23.1 %collective-permute-start.1 = (bf16[8,1,2048]{2,0,1:T(8,128)(2,1)S(1)}, bf16[8,1,2048]{2,0,1:T(8,128)(2,1)S(1)}, u32[]{:S(2)}, u32[]{:S(2)}) collective-permute-start(bf16[8,1,2048]{2,0,1:T(8,128)(2,1)S(1)} %pad_maximum_fusion.3), channel_id=1, source_target_pairs={{0,28},{2,30},{4,0},{6,2},{8,4},{10,6},{12,8},{14,10},{16,12},{18,... | collective-permute-start | bytes 98312 | tf_op jit(solution)/shard_map/ppermute | solution.py:22
  94.5 4.4 %collective-permute-start.2 = (bf16[16,1,2048]{2,0,1:T(8,128)(2,1)S(1)}, bf16[16,1,2048]{2,0,1:T(8,128)(2,1)S(1)}, u32[]{:S(2)}, u32[]{:S(2)}) collective-permute-start(bf16[16,1,2048]{2,0,1:T(8,128)(2,1)S(1)} %pad_maximum_fusion.2), channel_id=1, source_target_pairs={{0,24},{2,26},{4,28},{6,30},{8,0},{10,2},{12,4},{14,6},{16,8},{18,... | collective-permute-start | bytes 196616 | tf_op jit(solution)/shard_map/ppermute | solution.py:22
  98.9 8.4 %collective-permute-start.3 = (bf16[32,1,2048]{2,0,1:T(8,128)(2,1)S(1)}, bf16[32,1,2048]{2,0,1:T(8,128)(2,1)S(1)}, u32[]{:S(2)}, u32[]{:S(2)}) collective-permute-start(bf16[32,1,2048]{2,0,1:T(8,128)(2,1)S(1)} %pad_maximum_fusion.1), channel_id=1, source_target_pairs={{0,16},{2,18},{4,20},{6,22},{8,24},{10,26},{12,28},{14,30},{16,0},... | collective-permute-start | bytes 393224 | tf_op jit(solution)/shard_map/ppermute | solution.py:22
Sparse Core Ops, SparseCore 0:
  149.3 97.4 reduce-scatter.1
